TPU v7x, 128 devices: a whole 4x4x4 slice. The times are simulated.
128 devices in a mesh: dec: 32 (over z, x, core), seq: 4 (over y).
Axes of the slice: x: 4, y: 4, z: 4, core: 2. Of those that a mesh axis runs over, the one named last changes fastest.
Arguments:
- hidden_states: bfloat16 [1024, 7168], P(('dec', 'seq')), may hold values from -6 to 6
- gate_scores: float32 [1024, 8], P(('dec', 'seq')), may hold values from -6 to 6
- expert_ids: int32 [1024, 8], P(('dec', 'seq')), may hold values from 0 to 31, all different within a row; in each aligned block of 8 rows (0 to 7, 8 to 15, ...) at most 4 rows name the same one
- w_gate: bfloat16 [32, 7168, 2048], P('dec', None, 'seq'), may hold values from -0.0625 to 0.0625
- w_up: bfloat16 [32, 7168, 2048], P('dec', None, 'seq'), may hold values from -0.0625 to 0.0625
- w_down: bfloat16 [32, 2048, 7168], P('dec', 'seq'), may hold values from -0.125 to 0.125
- prefill_cache: bfloat16 [32, 1024, 576], P('dec', 'seq'), may hold values from -6 to 6
- plan: int32 [32], replicated, may hold values from 0 to 31, each once
- prompt_len: int32 [32], replicated, may hold values from 1 to 1024, 16384 in all
Outputs:
- moe_out: bfloat16 [1024, 7168], P(('dec', 'seq'))
- handed_cache: bfloat16 [32, 1024, 576], P('dec', 'seq')
Inputs may be any that keep to these rules, and one draw needn't show every extreme that they name: `expert_ids`: each row names 8 different experts; among the rows of one device no expert is named more than 4 times. `plan`: each decode index is chosen by exactly one prefill group. `prompt_len`: some request has exactly 1024 prompt tokens.
All inputs are finite; a program needn't handle non-finite values.
Results may differ from a plain program's by a relative error of at most 0.0066.
Values may be sent and summed in bfloat16 or wider, within the bound.
A program may use at most 128 MiB of HBM per device.

v0:
```python
import jax
import jax.numpy as jnp
from jax import lax
from jax.sharding import PartitionSpec as P


def body(
    hidden_states, gate_scores, expert_ids, w_gate, w_up, w_down, prefill_cache, plan, prompt_len
):
    n_dec = lax.axis_size("dec")
    n_seq = lax.axis_size("seq")
    tok_rows, features = hidden_states.shape
    per_token = expert_ids.shape[1]
    capacity = min(tok_rows, 2 * tok_rows * per_token // n_dec)
    affinity = jax.nn.sigmoid(gate_scores)
    weight = 2.5 * affinity / jnp.sum(affinity, axis=1, keepdims=True)
    flat_ids = expert_ids.reshape(-1)
    one_hot = (flat_ids[:, None] == jnp.arange(n_dec, dtype=jnp.int32)[None, :]).astype(jnp.int32)
    earlier = jnp.cumsum(one_hot, axis=0) - one_hot
    slot_index = jnp.sum(earlier * one_hot, axis=1)
    target = flat_ids * capacity + slot_index
    placed = jnp.any(
        target.reshape(tok_rows, per_token)[:, :, None]
        == jnp.arange(n_dec * capacity, dtype=jnp.int32)[None, None, :],
        axis=1,
    ).astype(jnp.bfloat16)
    buffer = jnp.einsum(
        "tj,td->jd", placed, hidden_states, preferred_element_type=jnp.float32
    ).astype(jnp.bfloat16)
    buffer = buffer.reshape(n_dec, capacity, features)
    gate_local = w_gate[0]
    up_local = w_up[0]
    down_local = w_down[0]
    copies = jnp.broadcast_to(buffer[:, None], (n_dec, n_seq, capacity, features))
    copies = copies.reshape(n_dec * n_seq, capacity, features)
    arrived = lax.all_to_all(copies, ("dec", "seq"), split_axis=0, concat_axis=0, tiled=True)
    token_block = arrived.reshape(-1, features)
    gate_proj = jnp.dot(token_block, gate_local, preferred_element_type=jnp.float32)
    up_proj = jnp.dot(token_block, up_local, preferred_element_type=jnp.float32)
    hidden = (jax.nn.silu(gate_proj) * up_proj).astype(jnp.bfloat16)
    partial_value = jnp.dot(hidden, down_local, preferred_element_type=jnp.float32).astype(
        jnp.bfloat16
    )
    partial_value = partial_value.reshape(n_dec * n_seq, capacity, features)
    returned = lax.all_to_all(
        partial_value, ("dec", "seq"), split_axis=0, concat_axis=0, tiled=True
    )
    returned = returned.reshape(n_dec, n_seq, capacity, features)
    expert_out = jnp.sum(returned, axis=1, dtype=jnp.float32).astype(jnp.bfloat16)
    picked = jnp.take(expert_out.reshape(n_dec * capacity, features), target, axis=0)
    picked = picked.reshape(tok_rows, per_token, features)
    moe_out = jnp.sum(weight[:, :, None] * picked.astype(jnp.float32), axis=1).astype(jnp.bfloat16)
    index_dec = lax.axis_index("dec")
    index_seq = lax.axis_index("seq")
    indices = jnp.arange(n_dec, dtype=jnp.int32)
    inverse = jnp.sum(jnp.where(plan[None, :] == indices[:, None], indices[None, :], 0), axis=1)
    source_req = jnp.sum(jnp.where(indices == index_dec, inverse, 0))
    length = jnp.sum(jnp.where(indices == source_req, prompt_len, 0))
    cache_rows, latent_dim = (prefill_cache.shape[1], prefill_cache.shape[2])
    flattened = prefill_cache.reshape(1, cache_rows * latent_dim)
    shard_piece = lax.all_gather(flattened, "dec", axis=0, tiled=True)
    chosen = jnp.arange(shard_piece.shape[0], dtype=jnp.int32) == source_req
    kept = jnp.where(chosen[:, None], shard_piece, jnp.zeros((), shard_piece.dtype))
    received = jnp.sum(kept, axis=0, keepdims=True)
    received = received.reshape(1, cache_rows, latent_dim)
    position = index_seq * cache_rows + jnp.arange(cache_rows, dtype=jnp.int32)
    live_rows = position < length
    handed_cache = jnp.where(live_rows[None, :, None], received, jnp.zeros((), received.dtype))
    return (moe_out, handed_cache)


def solution(mesh):
    in_specs = (
        P(("dec", "seq"), None),
        P(("dec", "seq"), None),
        P(("dec", "seq"), None),
        P("dec", None, "seq"),
        P("dec", None, "seq"),
        P("dec", "seq", None),
        P("dec", "seq", None),
        P(),
        P(),
    )
    out_specs = (P(("dec", "seq"), None), P("dec", "seq", None))
    return jax.shard_map(body, mesh=mesh, in_specs=in_specs, out_specs=out_specs, check_vma=False)
```

profile of v0, /device:TPU:1, one launch (start us, length us, event | category | flops | bytes accessed | tf_op | source)
XLA Modules:
  0.0 308.1 jit_solution(16169676667074226487)
XLA Ops:
  7.2 0.8 reshape.128
  8.1 0.1 reduce_window_sum.11
  8.2 0.2 select_reduce_fusion
  8.4 0.7 compare_and_fusion
  9.2 0.7 convolution_convert_fusion.1
  9.9 1.7 broadcast_in_dim.69
  11.6 6.6 %broadcast_in_dim.70 = bf16[32,4,4,7168]{3,2,1,0:T(4,128)(2,1)} broadcast(bf16[32,4,7168]{2,1,0:T(4,128)(2,1)} %broadcast_in_dim.69), dimensions={0,2,3} | broadcast | bytes 9175040 | tf_op jit(solution)/shard_map/broadcast_in_dim | solution.py:34
  18.2 11.9 %all-to-all-start = ((bf16[128,4,7168]{2,1,0:T(4,128)(2,1)}), bf16[128,4,7168]{2,1,0:T(4,128)(2,1)}, u32[]{:S(2)}, u32[]{:S(2)}) async-start(bf16[128,4,7168]{2,1,0:T(4,128)(2,1)} %bitcast.35), calls=%async_computation | async-start | bytes 14680064 | tf_op jit(solution)/shard_map/all_to_all | solution.py:36
  30.2 0.2 copy.17
  30.4 1.2 reshape.143
  31.6 92.3 %all-to-all-done = bf16[128,4,7168]{2,1,0:T(4,128)(2,1)} async-done(((bf16[128,4,7168]{2,1,0:T(4,128)(2,1)}), bf16[128,4,7168]{2,1,0:T(4,128)(2,1)}, u32[]{:S(2)}, u32[]{:S(2)}) %all-to-all-start) | async-done | bytes 7340064 | tf_op jit(solution)/shard_map/all_to_all | solution.py:36
  124.0 12.2 %reshape.130 = bf16[512,7168]{1,0:T(8,128)(2,1)} reshape(bf16[128,4,7168]{2,1,0:T(4,128)(2,1)} %all-to-all-done) | data formatting | bytes 14680064 | tf_op jit(solution)/shard_map/reshape | solution.py:37
  136.2 9.3 %fusion.4 = f32[512,512]{1,0:T(8,128)S(1)} fusion(bf16[512,7168]{1,0:T(8,128)(2,1)} %reshape.130, bf16[1,7168,512]{2,1,0:T(8,128)(2,1)} %param.12), kind=kOutput, calls=%fused_computation.9 | convolution fusion | flops 3758096384 | bytes 15728640 | tf_op jit(solution)/shard_map/dot_general | solution.py:38
  145.5 7.6 %fusion.9 = bf16[512,512]{1,0:T(8,128)(2,1)S(1)} fusion(bf16[512,7168]{1,0:T(8,128)(2,1)S(1)} %copy-done.2, bf16[1,7168,512]{2,1,0:T(8,128)(2,1)} %param.13, f32[512,512]{1,0:T(8,128)S(1)} %fusion.4), kind=kOutput, calls=%fused_computation.13 | convolution fusion | flops 3759669248 | bytes 16252928 | tf_op jit(solution)/shard_map/dot_general | solution.py:39
  153.0 9.6 %convolution_convert_fusion = bf16[512,7168]{1,0:T(8,128)(2,1)} fusion(bf16[512,512]{1,0:T(8,128)(2,1)S(1)} %fusion.9, bf16[1,512,7168]{2,1,0:T(8,128)(2,1)} %param.14), kind=kOutput, calls=%fused_computation.1 | convolution fusion | flops 3761766400 | bytes 15204352 | tf_op jit(solution)/shard_map/dot_general | solution.py:41
  162.6 12.7 %reshape.131 = bf16[128,4,7168]{2,1,0:T(4,128)(2,1)} reshape(bf16[512,7168]{1,0:T(8,128)(2,1)} %convolution_convert_fusion) | data formatting | bytes 14680064 | tf_op jit(solution)/shard_map/reshape | solution.py:44
  175.3 8.6 %all-to-all-start.1 = ((bf16[128,4,7168]{2,1,0:T(4,128)(2,1)}), bf16[128,4,7168]{2,1,0:T(4,128)(2,1)}, u32[]{:S(2)}, u32[]{:S(2)}) async-start(bf16[128,4,7168]{2,1,0:T(4,128)(2,1)} %reshape.131), calls=%async_computation.1 | async-start | bytes 14680064 | tf_op jit(solution)/shard_map/all_to_all | solution.py:45
  184.0 0.1 select_reduce_fusion.1
  184.1 0.6 fusion.15
  184.8 0.6 iota_compare_fusion.3
  185.5 1.3 select_reduce_fusion.2
  186.7 0.7 add_compare_fusion
  187.4 0.1 fusion.14
  187.6 83.2 %all-to-all-done.1 = bf16[128,4,7168]{2,1,0:T(4,128)(2,1)} async-done(((bf16[128,4,7168]{2,1,0:T(4,128)(2,1)}), bf16[128,4,7168]{2,1,0:T(4,128)(2,1)}, u32[]{:S(2)}, u32[]{:S(2)}) %all-to-all-start.1) | async-done | bytes 7340064 | tf_op jit(solution)/shard_map/all_to_all | solution.py:45
  270.8 8.9 %bitcast_reduce_fusion = bf16[32,4,7168]{2,1,0:T(4,128)(2,1)} fusion(bf16[128,4,7168]{2,1,0:T(4,128)(2,1)} %all-to-all-done.1), kind=kLoop, calls=%fused_computation.5 | loop fusion | flops 2752512 | bytes 9175040 | tf_op jit(solution)/shard_map/reduce_sum | solution.py:49
  279.7 2.9 reshape.133
  282.6 1.1 gather_fusion
  283.8 1.4 multiply_reduce_fusion
  285.1 14.8 %fusion = bf16[147456]{0:T(1024)(128)(2,1)S(1)} fusion(bf16[32,1,147456]{2,1,0:T(2,128)(2,1)} %all-gather.3.cloned.1.call-done, pred[32]{0:T(512)(128)(4,1)S(1)} %iota_compare_fusion.3), kind=kLoop, calls=%fused_computation.3 | loop fusion | flops 9289728 | bytes 9732128 | tf_op jit(solution)/shard_map/reduce_sum | solution.py:64
  300.0 0.3 convert_element_type.42
  300.2 0.1 broadcast_select_fusion
  300.4 0.9 copy.18
  (27 shorter events, 0.5 us)
Async XLA Ops:
  7.2 2.1 copy-start
  18.2 12.0 %copy-start.3 = (bf16[1,256,576]{1,2,0:T(8,128)(2,1)S(1)}, bf16[1,256,576]{1,2,0:T(8,128)(2,1)}, u32[]{:S(2)}) copy-start(bf16[1,256,576]{1,2,0:T(8,128)(2,1)} %param.15) | copy-start | bytes 884740
  18.2 105.7 %all-to-all-start = ((bf16[128,4,7168]{2,1,0:T(4,128)(2,1)}), bf16[128,4,7168]{2,1,0:T(4,128)(2,1)}, u32[]{:S(2)}, u32[]{:S(2)}) async-start(bf16[128,4,7168]{2,1,0:T(4,128)(2,1)} %bitcast.35), calls=%async_computation | async-start | bytes 14680064 | tf_op jit(solution)/shard_map/all_to_all | solution.py:36
  30.1 255.0 %all-gather.3.cloned.1.call-start = ((), (), s32[]{:S(2)}) async-start(), calls=%async_computation.2 | async-start | bytes 19464192 | tf_op jit(solution)/shard_map/all_gather | solution.py:61
  136.2 9.3 %copy-start.2 = (bf16[512,7168]{1,0:T(8,128)(2,1)S(1)}, bf16[512,7168]{1,0:T(8,128)(2,1)}, u32[]{:S(2)}) copy-start(bf16[512,7168]{1,0:T(8,128)(2,1)} %reshape.130) | copy-start | bytes 22020100
  175.3 8.6 %copy-start.4 = (s32[8,8]{1,0:T(8,128)S(1)}, s32[8,8]{1,0:T(8,128)}, u32[]{:S(2)}) copy-start(s32[8,8]{1,0:T(8,128)} %param.11) | copy-start | bytes 772
  175.3 8.7 %copy-start.6 = (s32[32]{0:T(128)S(1)}, s32[32]{0:T(128)}, u32[]{:S(2)}) copy-start(s32[32]{0:T(128)} %param.16) | copy-start | bytes 388
  175.3 10.1 %copy-start.7 = (s32[32]{0:T(128)S(1)}, s32[32]{0:T(128)}, u32[]{:S(2)}) copy-start(s32[32]{0:T(128)} %param.17) | copy-start | bytes 388
  175.3 12.1 %copy-start.5 = (f32[8,8]{1,0:T(8,128)S(1)}, f32[8,8]{1,0:T(8,128)}, u32[]{:S(2)}) copy-start(f32[8,8]{1,0:T(8,128)} %param.10) | copy-start | bytes 772
  175.3 95.4 %all-to-all-start.1 = ((bf16[128,4,7168]{2,1,0:T(4,128)(2,1)}), bf16[128,4,7168]{2,1,0:T(4,128)(2,1)}, u32[]{:S(2)}, u32[]{:S(2)}) async-start(bf16[128,4,7168]{2,1,0:T(4,128)(2,1)} %reshape.131), calls=%async_computation.1 | async-start | bytes 14680064 | tf_op jit(solution)/shard_map/all_to_all | solution.py:45
  283.8 17.5 %copy-start.1 = (bf16[8,7168]{1,0:T(8,128)(2,1)S(1)}, bf16[8,7168]{1,0:T(8,128)(2,1)}, u32[]{:S(2)}) copy-start(bf16[8,7168]{1,0:T(8,128)(2,1)} %param.9) | copy-start | bytes 344068
Sparse Core Ops, SparseCore 0:
  33.2 139.8 all-gather.2
where the time goes:
time: 311 us; the launch traced here: 308 us
  waiting for transfers between devices  176 us (57%)
  local copies, waits for them, and re-layouts  40.9 us (13%)
  other arithmetic  29.9 us (10%)
  matrix products  27.1 us (9%)
  starting transfers between devices  20.5 us (7%)
  between operations  14.2 us (5%)
    all_to_all x1, waiting for transfers between devices, body(): lax.all_to_all(copies, ('dec', 'seq'), split_axis=0, concat_axis=0, tiled...  92.3 us
    all_to_all x1, waiting for transfers between devices, body(): lax.all_to_all(partial_value, ('dec', 'seq'), split_axis=0, concat_axis=0...  83.2 us
    reduce_sum x1, other arithmetic, body(): received = jnp.sum(kept, axis=0, keepdims=True)  14.8 us
    reshape x1, local copies, waits for them, and re-layouts, body(): partial_value = partial_value.reshape(n_dec * n_seq, capacity, features)  12.7 us
    reshape x1, local copies, waits for them, and re-layouts, body(): token_block = arrived.reshape(-1, features)  12.2 us
    all_to_all x1, starting transfers between devices, body(): lax.all_to_all(copies, ('dec', 'seq'), split_axis=0, concat_axis=0, tiled...  11.9 us
    dot_general x1, matrix products, body(): jnp.dot(hidden, down_local, preferred_element_type=jnp.float32)  9.59 us
    dot_general x1, matrix products, body(): jnp.dot(token_block, gate_local, preferred_element_type=jnp.float32)  9.25 us
  transfers between devices with their start and end apart: 3, of which 2 were waited for; matrix products, arithmetic and copies ran while one was open for 23% of the time, Pallas kernels for 0%

commit v1 on v0

v1 whole, which is shorter than its diff:
```python
import jax
import jax.numpy as jnp
from jax import lax
from jax.experimental import pallas as pl
from jax.experimental.pallas import tpu as pltpu
from jax.sharding import PartitionSpec as P

MESH = pl.DeviceIdType.MESH
AX = ("z", "x", "y")
ORDER = (("y", "x", "z"), ("z", "y", "x"), ("x", "z", "y"))
NCH = 15
NOUT = 14
LANES = 256
SLOTS = 6
bf16 = jnp.bfloat16
f32 = jnp.float32


def mod4(v):
    return lax.rem(v + 8, 4)


def kernel(
    inv_ref, xin_ref, cache_ref, wg_ref, wu_ref, wd_ref,
    fo_ref, co_ref,
    X, xr, Wgu, Wd, acc, H, wb, R, RA1, RA2, T, RB1, RB2, U, RC1, RC2, C1, C2,
    x_sem, ag_s, ag_r, ag3_s, ag3_r, agp_s, agp_r, w_sem, wd_sem,
    rp_s, rp_r, rs_s, rs_r, fo_sem, c1_s, c1_r, cp_sem, c2_s, c2_r,
):
    dec = lax.axis_index("dec")
    y = lax.axis_index("seq")
    c = lax.rem(dec, 2)
    chip = dec // 2
    me = {"z": dec // 8, "x": lax.rem(dec // 2, 4), "y": y}

    def dev(pos, core):
        return ((pos["z"] * 4 + pos["x"]) * 2 + core, pos["y"])

    def neighbour(a, d):
        pos = dict(me)
        pos[a] = mod4(me[a] + d)
        return dev(pos, c)

    partner = dev(me, 1 - c)

    def plane_id(o):
        return (lax.rem(chip + o, 16) * 2 + c, y)

    def w_copies(i, g):
        n = 3 * i + g
        slot = lax.rem(n, SLOTS)
        j = 5 * g + i
        out = []
        for h in range(2):
            half = c if h == 0 else 1 - c
            row = pl.multiple_of(half * 3584 + j * LANES, LANES)
            for m, src in enumerate((wg_ref, wu_ref)):
                out.append(pltpu.make_async_copy(
                    src.at[0, pl.ds(row, LANES), :],
                    Wgu.at[slot, pl.ds(h * LANES, LANES), pl.ds(m * 512, 512)],
                    w_sem.at[slot, 2 * h + m]))
        return out

    def wd_copies(j):
        out = []
        for h in range(2):
            half = c if h == 0 else 1 - c
            col = pl.multiple_of(half * 3584 + j * LANES, LANES)
            out.append(pltpu.make_async_copy(
                wd_ref.at[0, :, pl.ds(col, LANES)],
                Wd.at[j, :, pl.ds(h * LANES, LANES)],
                wd_sem.at[j, h]))
        return out

    for i in range(2):
        for g in range(3):
            for cp in w_copies(i, g):
                cp.start()

    barrier = pltpu.get_barrier_semaphore()
    for o in range(1, 16):
        pl.semaphore_signal(barrier, inc=1, device_id=plane_id(o), device_id_type=MESH)
    for d in (1, -1):
        pl.semaphore_signal(barrier, inc=1, device_id=neighbour("y", d), device_id_type=MESH)
    pl.semaphore_signal(barrier, inc=1, device_id=partner, device_id_type=MESH)
    pl.semaphore_wait(barrier, 18)

    swap = pltpu.make_async_remote_copy(
        xin_ref.at[1 - c], xr, x_sem.at[0], x_sem.at[1], device_id=partner, device_id_type=MESH)
    swap.start()

    def wd_start(j, _):
        for cp in wd_copies(j):
            cp.start()
        return 0

    lax.fori_loop(0, NOUT, wd_start, 0)
    swap.wait()
    for j in range(NCH):
        lane = slice(j * LANES, (j + 1) * LANES)
        X[j, me["z"], me["x"], me["y"], :, 0:LANES] = xin_ref[c, :, lane] + xr[:, lane]

    def ag_copy(g, stage, kind, i=0):
        a = ORDER[g][stage]
        done = [b for b in AX if b in ORDER[g][:stage]]
        spec = {b: (slice(None) if b in done else me[b]) for b in AX}
        spec[a] = mod4(me[a] + (0, 0, -1, 1)[kind])
        lanes = pl.ds(0, LANES)
        if kind >= 2:
            if stage == 0:
                lanes = pl.ds((kind - 2) * 128, 128)
            else:
                spec[done[0]] = pl.ds((kind - 2) * 2, 2)
        if stage < 2:
            rows, s, r = pl.ds(5 * g, 5), ag_s.at[stage, g, kind], ag_r.at[stage, g, kind]
        else:
            j = 5 * g + i
            rows, s, r = j, ag3_s.at[j, kind], ag3_r.at[j, kind]
        ref = X.at[rows, spec["z"], spec["x"], spec["y"], :, lanes]
        return pltpu.make_async_remote_copy(
            ref, ref, s, r, device_id=neighbour(a, 1 if kind % 2 == 0 else -1), device_id_type=MESH)

    def ag_partner(j):
        return pltpu.make_async_remote_copy(
            X.at[j, :, :, :, :, pl.ds(0, LANES)], X.at[j, :, :, :, :, pl.ds(LANES, LANES)],
            agp_s.at[j], agp_r.at[j], device_id=partner, device_id_type=MESH)

    def c1_copy(o):
        to = lax.rem(chip + o, 16)
        return pltpu.make_async_remote_copy(
            cache_ref.at[to], C1.at[chip], c1_s.at[o], c1_r.at[o],
            device_id=plane_id(o), device_id_type=MESH)

    def c2_copy(o):
        to = lax.rem(chip + o, 16)
        return pltpu.make_async_remote_copy(
            C2.at[to], co_ref.at[chip], c2_s.at[o], c2_r.at[o],
            device_id=plane_id(o), device_id_type=MESH)

    for stage in range(2):
        for g in range(3):
            for kind in range(2):
                ag_copy(g, stage, kind).start()
        if stage == 1:
            def c1_start(o, _):
                c1_copy(o).start()
                return 0

            lax.fori_loop(1, 16, c1_start, 0)
            C1[chip] = cache_ref[chip]
            acc[...] = jnp.zeros_like(acc)
        for g in range(3):
            for kind in range(2):
                ag_copy(g, stage, kind).wait_recv()
                ag_copy(g, stage, kind + 2).start()
        for g in range(3):
            for kind in range(2):
                ag_copy(g, stage, kind + 2).wait_recv()

    def ag3_start(i, _):
        for g in range(3):
            for kind in range(2):
                ag_copy(g, 2, kind, i).start()
        return 0

    lax.fori_loop(0, 5, ag3_start, 0)

    def valid(i, g, top=5):
        return (i >= 0) & (i < (4 if g == 2 else top))

    def gate_up(i, g):
        j = 5 * g + i
        slot = lax.rem(3 * i + g, SLOTS)
        for cp in w_copies(i, g):
            cp.wait()

        def rows(zi, _):
            xb = X[j, zi].reshape(256, 512)
            acc[zi] += jnp.dot(xb, Wgu[slot], preferred_element_type=f32)
            return 0

        lax.fori_loop(0, 4, rows, 0)

        @pl.when(valid(i + 2, g))
        def _():
            for cp in w_copies(i + 2, g):
                cp.start()

    def ag_step(i, _):
        for g in range(3):
            @pl.when(i < 5)
            def _():
                for kind in range(2):
                    ag_copy(g, 2, kind, i).wait_recv()
                    ag_copy(g, 2, kind + 2, i).start()
        for g in range(3):
            @pl.when((i >= 1) & (i < 6))
            def _():
                for kind in range(2):
                    ag_copy(g, 2, kind + 2, i - 1).wait_recv()

            @pl.when(valid(i - 1, g))
            def _():
                ag_partner(5 * g + i - 1).start()
        for g in range(3):
            @pl.when(valid(i - 2, g))
            def _():
                ag_partner(5 * g + i - 2).wait_recv()
                gate_up(i - 2, g)

        @pl.when(i == 3)
        def _():
            def c1_wait(o, _):
                c1_copy(o).wait_recv()
                return 0

            lax.fori_loop(1, 16, c1_wait, 0)
            cp_copy().start()

        return 0

    def cp_copy():
        return pltpu.make_async_remote_copy(
            C1.at[pl.ds(0, 16)], C1.at[pl.ds(16, 16)], cp_sem.at[0], cp_sem.at[1],
            device_id=partner, device_id_type=MESH)

    lax.fori_loop(0, 7, ag_step, 0)

    cp_copy().wait()

    def reorder(k, _):
        C2[k] = C1[inv_ref[k]]
        return 0

    lax.fori_loop(0, 16, reorder, 0)

    def c2_start(o, _):
        c2_copy(o).start()
        return 0

    lax.fori_loop(1, 16, c2_start, 0)
    co_ref[chip] = C2[chip]

    for g in range(3):
        for kind in range(4):
            for stage in range(2):
                ag_copy(g, stage, kind).wait_send()

    def ag_drain(i, _):
        for g in range(3):
            for kind in range(4):
                ag_copy(g, 2, kind, i).wait_send()

            @pl.when(valid(i, g))
            def _():
                ag_partner(5 * g + i).wait_send()
        return 0

    lax.fori_loop(0, 5, ag_drain, 0)

    lane_id = lax.broadcasted_iota(jnp.int32, (128, 128), 0)
    pick = jnp.where((lax.rem(lane_id, 32) == dec) & (lane_id < 96), 1.0, 0.0).astype(bf16)

    def hidden_rows(zi, _):
        gate = acc[zi, :, 0:512]
        up = acc[zi, :, 512:1024]
        H[zi] = (gate / (1.0 + jnp.exp(-gate)) * up).astype(bf16)
        wb[zi] = jnp.dot(X[14, zi, :, :, :, 0:128].reshape(256, 128), pick,
                         preferred_element_type=f32)
        return 0

    lax.fori_loop(0, 4, hidden_rows, 0)

    def rp_copy(j):
        return pltpu.make_async_remote_copy(
            X.at[j, :, :, :, :, pl.ds(LANES, LANES)], R.at[j], rp_s.at[j], rp_r.at[j],
            device_id=partner, device_id_type=MESH)

    def down(i, g):
        j = 5 * g + i
        for cp in wd_copies(j):
            cp.wait()

        def rows(zi, _):
            part = jnp.dot(H[zi], Wd[j], preferred_element_type=f32)
            w = wb[zi]
            part = part * jnp.concatenate([w, w, w, w], axis=1)
            X[j, zi] = part.astype(bf16).reshape(4, 4, 16, 512)
            return 0

        lax.fori_loop(0, 4, rows, 0)
        rp_copy(j).start()

    def chip_sum(j):
        rp_copy(j).wait_recv()

        def rows(zi, _):
            own = X[j, zi, :, :, :, 0:LANES].astype(f32)
            X[j, zi, :, :, :, 0:LANES] = (own + R[j, zi].astype(f32)).astype(bf16)
            return 0

        lax.fori_loop(0, 4, rows, 0)

    def part_of(g, stage, j, at, half=None):
        a1, a2, a3 = ORDER[g]
        hs = slice(None) if half is None else pl.ds(2 * half, 2)
        if stage == 0:
            spec = {b: slice(None) for b in AX}
            rest = [b for b in AX if b != a3]
            spec[a3], spec[rest[0]] = at, hs
            return X.at[j, spec["z"], spec["x"], spec["y"], :, pl.ds(0, LANES)]
        if stage == 1:
            rest = [b for b in AX if b != a3]
            if rest[0] == a2:
                return T.at[j, at, hs]
            return T.at[j, hs, at]
        if half is None:
            return U.at[j, at]
        return U.at[j, at, :, pl.ds(128 * half, 128)]

    first = (RA1, RB1, RC1)
    second = (RA2, RB2, RC2)
    result = (T, U, fo_ref.at[0])

    def rs_copy(g, stage, kind, j):
        a = ORDER[g][2 - stage]
        p = me[a]
        if kind < 2:
            src, dst = part_of(g, stage, j, mod4(p + 2), kind), first[stage].at[kind, j]
        else:
            src = part_of(g, stage, j, mod4(p + (1 if kind == 2 else -1)))
            dst = second[stage].at[kind - 2, j]
        return pltpu.make_async_remote_copy(
            src, dst, rs_s.at[j, stage, kind], rs_r.at[j, stage, kind],
            device_id=neighbour(a, 1 if kind % 2 == 0 else -1), device_id_type=MESH)

    def rs_first(g, stage, j):
        for kind in range(2):
            rs_copy(g, stage, kind, j).start()

    def rs_second(g, stage, j):
        p = me[ORDER[g][2 - stage]]
        for kind in range(2):
            rs_copy(g, stage, kind, j).wait_recv()
            ref = part_of(g, stage, j, mod4(p + (1 if kind == 0 else -1)), kind)
            ref[...] = (ref[...].astype(f32) + first[stage][kind, j].astype(f32)).astype(bf16)
            rs_copy(g, stage, kind + 2, j).start()

    def rs_last(g, stage, j):
        p = me[ORDER[g][2 - stage]]
        for kind in range(2):
            rs_copy(g, stage, kind + 2, j).wait_recv()
        total = (part_of(g, stage, j, p)[...].astype(f32) + second[stage][0, j].astype(f32)
                 + second[stage][1, j].astype(f32))
        result[stage][j] = total.astype(bf16)

    def rs_step(i, _):
        for g in range(3):
            @pl.when(valid(i, g))
            def _():
                down(i, g)
        for g in range(3):
            @pl.when(valid(i, g))
            def _():
                chip_sum(5 * g + i)
                rs_first(g, 0, 5 * g + i)
        for stage in range(3):
            lag = 1 + 2 * stage
            for g in range(3):
                @pl.when(valid(i - lag, g))
                def _():
                    rs_second(g, stage, 5 * g + i - lag)
            for g in range(3):
                @pl.when(valid(i - lag - 1, g))
                def _():
                    rs_last(g, stage, 5 * g + i - lag - 1)
                    if stage < 2:
                        rs_first(g, stage + 1, 5 * g + i - lag - 1)
        return 0

    lax.fori_loop(0, 11, rs_step, 0)

    fo = pltpu.make_async_remote_copy(
        fo_ref.at[0], fo_ref.at[1], fo_sem.at[0], fo_sem.at[1],
        device_id=partner, device_id_type=MESH)
    fo.start()

    def c_drain(o, _):
        c1_copy(o).wait_send()
        c2_copy(o).wait()
        return 0

    lax.fori_loop(1, 16, c_drain, 0)

    def rs_drain(i, _):
        for g in range(3):
            @pl.when(valid(i, g))
            def _():
                j = 5 * g + i
                rp_copy(j).wait_send()
                for stage in range(3):
                    for kind in range(4):
                        rs_copy(g, stage, kind, j).wait_send()
        return 0

    lax.fori_loop(0, 5, rs_drain, 0)
    fo.wait()


def body(
    hidden_states, gate_scores, expert_ids, w_gate, w_up, w_down, prefill_cache, plan, prompt_len
):
    dec = lax.axis_index("dec")
    seq = lax.axis_index("seq")
    core = lax.rem(dec, 2)
    n_dec = 32

    affinity = jax.nn.sigmoid(gate_scores)
    weight = 2.5 * affinity / jnp.sum(affinity, axis=1, keepdims=True)
    experts = jnp.arange(n_dec, dtype=jnp.int32)
    dense = jnp.sum(
        jnp.where(expert_ids[:, :, None] == experts[None, None, :], weight[:, :, None], 0.0), axis=1)
    hi = lax.reduce_precision(dense, 8, 7)
    mid = lax.reduce_precision(dense - hi, 8, 7)
    low = dense - hi - mid
    zeros = jnp.zeros((8, 160), f32)
    extra = jnp.concatenate([hi, mid, low, zeros], axis=1).astype(bf16)
    halves = jnp.stack([
        jnp.concatenate([hidden_states[:, :3584], extra], axis=1),
        jnp.concatenate([hidden_states[:, 3584:], extra], axis=1)])
    both = jnp.concatenate([halves, halves], axis=1)
    mine = lax.broadcasted_iota(jnp.int32, both.shape, 1) // 8 == core
    xin = jnp.where(mine, both, jnp.zeros((), bf16))

    indices = jnp.arange(n_dec, dtype=jnp.int32)
    inverse = jnp.sum(jnp.where(plan[None, :] == indices[:, None], indices[None, :], 0), axis=1)
    length = jnp.sum(jnp.where(plan == dec, prompt_len, 0))
    of_core = jnp.where(core == 0, inverse[0::2], inverse[1::2])
    order = lax.rem(lax.rem(of_core, 2) + core, 2) * 16 + of_core // 2

    vm = pl.BlockSpec(memory_space=pltpu.VMEM)
    hbm = pl.BlockSpec(memory_space=pl.ANY)
    dma = pltpu.SemaphoreType.DMA
    fo, co = pl.pallas_call(
        kernel,
        out_shape=(
            jax.ShapeDtypeStruct((2, NOUT, 16, LANES), bf16),
            jax.ShapeDtypeStruct((16, 16, 576), bf16),
        ),
        in_specs=[pl.BlockSpec(memory_space=pltpu.SMEM), vm, vm, hbm, hbm, hbm],
        out_specs=(vm, vm),
        scratch_shapes=[
            pltpu.VMEM((NCH, 4, 4, 4, 16, 512), bf16),
            pltpu.VMEM((16, NCH * LANES), bf16),
            pltpu.VMEM((SLOTS, 512, 1024), bf16),
            pltpu.VMEM((NOUT, 512, 512), bf16),
            pltpu.VMEM((4, 256, 1024), f32),
            pltpu.VMEM((4, 256, 512), bf16),
            pltpu.VMEM((4, 256, 128), f32),
            pltpu.VMEM((NOUT, 4, 4, 4, 16, LANES), bf16),
            pltpu.VMEM((2, NOUT, 2, 4, 16, LANES), bf16),
            pltpu.VMEM((2, NOUT, 4, 4, 16, LANES), bf16),
            pltpu.VMEM((NOUT, 4, 4, 16, LANES), bf16),
            pltpu.VMEM((2, NOUT, 2, 16, LANES), bf16),
            pltpu.VMEM((2, NOUT, 4, 16, LANES), bf16),
            pltpu.VMEM((NOUT, 4, 16, LANES), bf16),
            pltpu.VMEM((2, NOUT, 16, 128), bf16),
            pltpu.VMEM((2, NOUT, 16, LANES), bf16),
            pltpu.VMEM((32, 16, 576), bf16),
            pltpu.VMEM((16, 16, 576), bf16),
            dma((2,)),
            dma((2, 3, 4)), dma((2, 3, 4)),
            dma((NCH, 4)), dma((NCH, 4)),
            dma((NCH,)), dma((NCH,)),
            dma((SLOTS, 4)), dma((NOUT, 2)),
            dma((NOUT,)), dma((NOUT,)),
            dma((NOUT, 3, 4)), dma((NOUT, 3, 4)),
            dma((2,)),
            dma((16,)), dma((16,)),
            dma((2,)),
            dma((16,)), dma((16,)),
        ],
        compiler_params=pltpu.CompilerParams(
            collective_id=0, has_side_effects=True, vmem_limit_bytes=60 * 1024 * 1024),
        cost_estimate=pl.CostEstimate(
            flops=22_500_000_000, bytes_accessed=23_000_000, transcendentals=524288),
    )(order, xin, prefill_cache.reshape(16, 16, 576), w_gate, w_up, w_down)

    rows = jnp.where(core == 0, fo[:, :, :8], fo[:, :, 8:])
    rows = jnp.transpose(rows, (2, 0, 1, 3)).reshape(8, 2, 3584)
    moe_out = jnp.where(core == 0, rows, rows[:, ::-1]).reshape(8, 7168)

    position = seq * 256 + jnp.arange(256, dtype=jnp.int32)
    handed = co.reshape(1, 256, 576)
    handed_cache = jnp.where((position < length)[None, :, None], handed, jnp.zeros((), bf16))
    return (moe_out, handed_cache)


def solution(mesh):
    in_specs = (
        P(("dec", "seq"), None),
        P(("dec", "seq"), None),
        P(("dec", "seq"), None),
        P("dec", None, "seq"),
        P("dec", None, "seq"),
        P("dec", "seq", None),
        P("dec", "seq", None),
        P(),
        P(),
    )
    out_specs = (P(("dec", "seq"), None), P("dec", "seq", None))
    return jax.shard_map(body, mesh=mesh, in_specs=in_specs, out_specs=out_specs, check_vma=False)
```

time: 311 us -> 147 us (0.47)
  waiting for transfers between devices: 176 us -> 0 us
  Pallas kernels: 0 us -> 133 us
  local copies, waits for them, and re-layouts: 40.9 us -> 4.22 us
  matrix products: 27.1 us -> 0 us
  other arithmetic: 29.9 us -> 8.81 us
  starting transfers between devices: 20.5 us -> 0 us
  between operations: 14.2 us -> 0.7 us
    all_to_all x2 -> x0, waiting for transfers between devices: 175 us -> none  [the longest x1 92.3 us: body(): lax.all_to_all(copies, ('dec', 'seq'), split_axis=0, concat_axis=0, tiled...]
    pallas_call x0 -> x1, Pallas kernels: none -> 133 us  [body(): pl.pallas_call(kernel, out_shape=(jax.ShapeDtypeStruct((2, NOUT, 16, LANE...]
    reshape x4 -> x1, local copies, waits for them, and re-layouts: 28.7 us -> 1.12 us  [body(): handed = co.reshape(1, 256, 576)]
    dot_general x4 -> x0, matrix products: 27.1 us -> none  [the longest x1 9.59 us: body(): jnp.dot(hidden, down_local, preferred_element_type=jnp.float32)]
    reduce_sum x6 -> x2, other arithmetic: 27.2 us -> 2.1 us  [the longest x1 1.31 us: body(): length = jnp.sum(jnp.where(plan == dec, prompt_len, 0))]
    all_to_all x2 -> x0, starting transfers between devices: 20.5 us -> none  [the longest x1 11.9 us: body(): lax.all_to_all(copies, ('dec', 'seq'), split_axis=0, concat_axis=0, tiled...]
    broadcast_in_dim x2 -> x1, local copies, waits for them, and re-layouts: 8.3 us -> 0.01 us  [body(): zeros = jnp.zeros((8, 160), f32)]
  transfers between devices with their start and end apart: 3 -> 0, of which waited for: 2 -> 0; matrix products, arithmetic and copies ran while one was open for 23% -> 0% of each run, Pallas kernels for 0% -> 0%
where the time goes in v1:
time: 147 us
  Pallas kernels  133 us (90%)
  other arithmetic  8.81 us (6%)
  local copies, waits for them, and re-layouts  4.22 us (3%)
    pallas_call x1, Pallas kernels, body(): pl.pallas_call(kernel, out_shape=(jax.ShapeDtypeStruct((2, NOUT, 16, LANE...  133 us

profile of v1, /device:TPU:1, one launch (start us, length us, event | category | flops | bytes accessed | tf_op | source)
XLA Modules:
  0.0 146.9 jit_solution(15548612696110707686)
XLA Ops:
  0.6 1.3 fusion.3
  1.9 0.7 add_compare_fusion
  2.6 0.8 select_reduce_fusion.1
  3.4 0.1 slice.19
  3.5 0.1 slice.18
  3.6 0.5 fusion.6.inv_ref
  4.1 0.8 fusion.2
  5.0 0.8 multiply_divide_fusion
  5.7 0.8 select_reduce_fusion
  6.5 0.9 fusion.7
  7.4 0.1 concatenate.13
  7.5 0.1 concatenate.14
  7.6 0.8 fusion.xin_ref
  8.4 1.8 %copy.13 = bf16[1,256,576]{2,1,0:T(8,128)(2,1)} copy(bf16[1,256,576]{1,2,0:T(8,128)(2,1)} %param.15) | data formatting | bytes 589824 | tf_op args[6]
  10.2 133.2 %shard_map.104 = (bf16[2,14,16,256]{3,2,1,0:T(8,128)(2,1)}, bf16[16,16,576]{2,1,0:T(8,128)(2,1)}) custom-call(s32[16]{0:T(128)} %fusion.6.inv_ref, bf16[2,16,3840]{2,1,0:T(8,128)(2,1)} %fusion.xin_ref, bf16[16,16,576]{2,1,0:T(8,128)(2,1)} %bitcast.10, bf16[1,7168,512]{2,1,0:T(8,128)(2,1)} %wg_ref.1, bf16[1,7168,512]{2,1,0:T(8,128)(2,1)} %wu_ref.1, ...), custom_call_target="tpu_custom_call" | custom-call | flops 22499999744 | bytes 23000000 | tf_op jit(solution)/shard_map/pallas_call | solution.py:444
  143.4 1.0 slice_select_fusion
  144.4 0.7 reverse_select_fusion
  145.1 1.1 copy.14
  146.2 0.7 broadcast_select_fusion
  (4 shorter events, 0.0 us)

commit v2 on v0

v2 whole, which is shorter than its diff:
```python
import jax
import jax.numpy as jnp
from jax import lax
from jax.experimental import pallas as pl
from jax.experimental.pallas import tpu as pltpu
from jax.sharding import PartitionSpec as P

MESH = pl.DeviceIdType.MESH
AX = ("z", "x", "y")
ORDER = (("y", "x", "z"), ("z", "y", "x"), ("x", "z", "y"))
NCH = 15
NOUT = 14
LANES = 256
HALF = NOUT * LANES
SLOTS = 6
PIECES = 12
bf16 = jnp.bfloat16
f32 = jnp.float32


def mod4(v):
    return lax.rem(v + 8, 4)


def loop(lo, hi, fn):
    def step(k, carry):
        fn(k)
        return carry

    lax.fori_loop(lo, hi, step, 0)


def kernel(
    plan_hbm, plen_hbm, scores_hbm, ids_hbm, hid_hbm, cache_ref, wg_ref, wu_ref, wd_ref,
    moe_hbm, co_hbm,
    X, xin, xr, Wgu, Wd, acc, H, wb, R, RA1, RA2, T, RB, U, RC, FS, FR, C1, C2, order_ref,
    plan_ref, plen_ref, scores_ref, ids_ref, hid_ref, moe_ref, co_ref, io_sem,
    x_sem, ag_s, ag_r, ag3_s, ag3_r, agp_s, agp_r, w_sem, wd_sem,
    rp_s, rp_r, rs_s, rs_r, rb_s, rb_r, fo_sem, c_sem, cp_sem,
):
    dec = lax.axis_index("dec")
    y = lax.axis_index("seq")
    c = lax.rem(dec, 2)
    chip = dec // 2
    me = {"z": dec // 8, "x": lax.rem(dec // 2, 4), "y": y}

    def dev(pos, core):
        return ((pos["z"] * 4 + pos["x"]) * 2 + core, pos["y"])

    def peer(a, d):
        pos = dict(me)
        pos[a] = mod4(me[a] + d)
        return dev(pos, c)

    partner = dev(me, 1 - c)

    def plane_id(o):
        return (lax.rem(chip + o, 16) * 2 + c, y)

    def remote(src, dst, s, r, to):
        return pltpu.make_async_remote_copy(src, dst, s, r, device_id=to, device_id_type=MESH)

    loads = [pltpu.make_async_copy(src, dst, io_sem.at[q]) for q, (src, dst) in enumerate((
        (hid_hbm, hid_ref), (scores_hbm, scores_ref), (ids_hbm, ids_ref),
        (plan_hbm, plan_ref), (plen_hbm, plen_ref)))]
    for cp in loads:
        cp.start()

    def take(sem, ref):
        pltpu.make_async_copy(ref, ref, sem).wait()

    barrier = pltpu.get_barrier_semaphore()
    for o in range(1, 16):
        pl.semaphore_signal(barrier, inc=1, device_id=plane_id(o), device_id_type=MESH)
    for d in (1, -1, 2):
        pl.semaphore_signal(barrier, inc=1, device_id=peer("y", d), device_id_type=MESH)
    pl.semaphore_signal(barrier, inc=1, device_id=partner, device_id_type=MESH)

    def w_copies(i, g):
        slot = lax.rem(3 * i + g, SLOTS)
        j = 5 * g + i
        out = []
        for h in range(2):
            half = c if h == 0 else 1 - c
            row = pl.multiple_of(half * HALF + j * LANES, LANES)
            for m, src in enumerate((wg_ref, wu_ref)):
                out.append(pltpu.make_async_copy(
                    src.at[0, pl.ds(row, LANES), :],
                    Wgu.at[slot, pl.ds(h * LANES, LANES), pl.ds(m * 512, 512)],
                    w_sem.at[slot]))
        return out

    def wd_copies(j):
        out = []
        for h in range(2):
            half = c if h == 0 else 1 - c
            col = pl.multiple_of(half * HALF + j * LANES, LANES)
            out.append(pltpu.make_async_copy(
                wd_ref.at[0, :, pl.ds(col, LANES)],
                Wd.at[j, :, pl.ds(h * LANES, LANES)],
                wd_sem.at[j]))
        return out

    for i in range(2):
        for g in range(3):
            for cp in w_copies(i, g):
                cp.start()

    for cp in loads:
        cp.wait()
    score = 1.0 / (1.0 + jnp.exp(-scores_ref[...]))
    weight = 2.5 * score / jnp.sum(score, axis=1, keepdims=True)
    ids = ids_ref[...]
    lane8 = lax.broadcasted_iota(jnp.int32, (8, 128), 1)
    dense = jnp.zeros((8, 128), f32)
    for k in range(8):
        dense += jnp.where(ids[:, k:k + 1] == lane8 % 32, weight[:, k:k + 1], 0.0)
    hi = dense.astype(bf16).astype(f32)
    mid = (dense - hi).astype(bf16).astype(f32)
    low = dense - hi - mid
    part = lane8 // 32
    extra = jnp.where(part == 0, hi, jnp.where(part == 1, mid, jnp.where(part == 2, low, 0.0)))

    def two(v):
        mine = lax.broadcasted_iota(jnp.int32, (16, v.shape[1]), 0) // 8 == c
        return jnp.where(mine, jnp.concatenate([v, v], axis=0), 0.0).astype(bf16)

    for h in range(2):
        for t in range(NOUT):
            lane = slice(h * HALF + t * LANES, h * HALF + (t + 1) * LANES)
            xin[h, :, t * LANES:(t + 1) * LANES] = two(hid_ref[:, lane].astype(f32))
        xin[h, :, HALF:HALF + 128] = two(extra)
        xin[h, :, HALF + 128:HALF + 256] = jnp.zeros((16, 128), bf16)

    pl.semaphore_wait(barrier, 19)

    swap = remote(xin.at[1 - c], xr, x_sem.at[0], x_sem.at[1], partner)
    swap.start()
    swap.wait()
    for j in range(NCH):
        lane = slice(j * LANES, (j + 1) * LANES)
        X[j, me["z"], me["x"], me["y"], :, 0:LANES] = xin[c, :, lane] + xr[:, lane]

    PEERS = (1, -1, 2)

    def ag_copy(g, stage, part, q):
        a = ORDER[g][stage]
        done = ORDER[g][:stage]
        spec = {b: (slice(None) if b in done else me[b]) for b in AX}
        rows = pl.ds(5 * g, 1) if part == 0 else pl.ds(5 * g + 1, 4)
        ref = X.at[rows, spec["z"], spec["x"], spec["y"], :, pl.ds(0, LANES)]
        return remote(ref, ref, ag_s.at[stage], ag_r.at[stage, part],
                      peer(a, PEERS[q]))

    def ag3_copy(g, kind, i):
        a = ORDER[g][2]
        done = [b for b in AX if b != a]
        spec = {b: slice(None) for b in AX}
        spec[a] = mod4(me[a] + (0, 0, -1, 1)[kind])
        if kind >= 2:
            spec[done[0]] = pl.ds((kind - 2) * 2, 2)
        j = 5 * g + i
        ref = X.at[j, spec["z"], spec["x"], spec["y"], :, pl.ds(0, LANES)]
        return remote(ref, ref, ag3_s, ag3_r.at[j, kind // 2],
                      peer(a, 1 if kind % 2 == 0 else -1))

    def ag_partner(j):
        return remote(
            X.at[j, :, :, :, :, pl.ds(0, LANES)], X.at[j, :, :, :, :, pl.ds(LANES, LANES)],
            agp_s, agp_r.at[j], partner)

    def piece(k):
        return pl.ds(pl.multiple_of(k * 48, 16), 48)

    serves = chip < PIECES

    def c1_copy(o):
        to = lax.rem(chip + o, 16)
        return remote(cache_ref.at[0, piece(to), :], C1.at[chip], c_sem.at[0], c_sem.at[1],
                      plane_id(o))

    def c2_copy(o):
        to = lax.rem(chip + o, 16)
        return remote(C2.at[to], co_ref.at[piece(chip), :], c_sem.at[2], c_sem.at[3],
                      plane_id(o))

    def cp_copy():
        return remote(C1.at[pl.ds(0, 16)], C1.at[pl.ds(16, 16)], cp_sem.at[0], cp_sem.at[1],
                      partner)

    def ag_all(stage, part, act):
        for g in range(3):
            for q in range(3):
                act(ag_copy(g, stage, part, q))

    def start(cp):
        cp.start()

    def ag_take(stage, part):
        ref = X.at[pl.ds(0, 9), 0, pl.ds(0, 4 ** part), pl.ds(0, 4 ** stage), :, pl.ds(0, LANES)]
        take(ag_r.at[stage, part], ref)

    def ag3_take(i, g, k):
        a = ORDER[g][2]
        spec = {b: slice(None) for b in AX}
        spec[a] = pl.ds(0, 2 - k)
        take(ag3_r.at[5 * g + i, k],
             X.at[5 * g + i, spec["z"], spec["x"], spec["y"], :, pl.ds(0, LANES)])

    ag_all(0, 0, start)
    ag_all(0, 1, start)

    def wd_start(j):
        for cp in wd_copies(j):
            cp.start()

    loop(0, NOUT, wd_start)
    acc[...] = jnp.zeros_like(acc)

    def find(k):
        d = 2 * k + c
        src = jnp.int32(0)
        for q in range(32):
            src = jnp.where(plan_ref[q] == d, jnp.int32(q), src)
        order_ref[k] = lax.rem(lax.rem(src, 2) + c, 2) * 16 + src // 2

    ag_take(0, 0)
    ag_all(1, 0, start)
    ag_take(0, 1)
    ag_all(1, 1, start)

    def c1_own():
        return pltpu.make_async_copy(cache_ref.at[0, piece(chip), :], C1.at[chip], c_sem.at[4])

    def c1_start(o):
        @pl.when(lax.rem(chip + o, 16) < PIECES)
        def _():
            c1_copy(o).start()

    loop(1, 16, c1_start)

    @pl.when(serves)
    def _():
        c1_own().start()

    loop(0, 16, find)

    def ag3_start(i):
        for g in range(3):
            for kind in range(2):
                ag3_copy(g, kind, i).start()

    ag_take(1, 0)
    ag3_start(0)
    ag_take(1, 1)
    ag3_start(1)

    def valid(i, g):
        return (i >= 0) & (i < (4 if g == 2 else 5))

    def gate_up(i, g):
        j = 5 * g + i
        slot = lax.rem(3 * i + g, SLOTS)
        take(w_sem.at[slot], Wgu.at[slot])

        for zi in range(4):
            xb = X[j, zi].reshape(256, 512)
            acc[zi] += jnp.dot(xb, Wgu[slot], preferred_element_type=f32)

        @pl.when(valid(i + 2, g))
        def _():
            for cp in w_copies(i + 2, g):
                cp.start()

    def ag_step(i):
        for g in range(3):
            @pl.when(i < 5)
            def _():
                ag3_take(i, g, 0)
                for kind in range(2):
                    ag3_copy(g, kind + 2, i).start()

            @pl.when(i + 2 < 5)
            def _():
                for kind in range(2):
                    ag3_copy(g, kind, i + 2).start()

            @pl.when(valid(i - 2, g))
            def _():
                ag_partner(5 * g + i - 2).wait_recv()
                gate_up(i - 2, g)

            @pl.when((i >= 1) & (i < 6))
            def _():
                ag3_take(i - 1, g, 1)

            @pl.when(valid(i - 1, g))
            def _():
                ag_partner(5 * g + i - 1).start()

        @pl.when(i == 2)
        def _():
            @pl.when(serves)
            def _():
                take(c_sem.at[1], C1.at[pl.ds(0, 15)])
                c1_own().wait()
                cp_copy().start()

        @pl.when(i == 5)
        def _():
            @pl.when(serves)
            def _():
                cp_copy().wait()

                def reorder(k):
                    C2[k] = C1[order_ref[k]]

                loop(0, 16, reorder)
                loop(1, 16, lambda o: c2_copy(o).start())
                co_ref[piece(chip), :] = C2[chip]

    loop(0, 7, ag_step)

    low_lanes = pl.ds(0, LANES)
    take(ag_s.at[0], X.at[:, 0, 0, pl.ds(0, 3), :, low_lanes])
    take(ag_s.at[1], X.at[:, 0, pl.ds(0, 3), :, :, low_lanes])
    take(ag3_s, X.at[:, pl.ds(0, 3), :, :, :, low_lanes])
    take(agp_s, X.at[pl.ds(0, NOUT), :, :, :, :, low_lanes])

    lane_id = lax.broadcasted_iota(jnp.int32, (128, 128), 0)
    pick = jnp.where((lax.rem(lane_id, 32) == dec) & (lane_id < 96), 1.0, 0.0).astype(bf16)

    def hidden_rows(zi):
        gate = acc[zi, :, 0:512]
        up = acc[zi, :, 512:1024]
        H[zi] = (gate / (1.0 + jnp.exp(-gate)) * up).astype(bf16)
        wb[zi] = jnp.dot(X[14, zi, :, :, :, 0:128].reshape(256, 128), pick,
                         preferred_element_type=f32)

    loop(0, 4, hidden_rows)

    def rp_copy(j):
        return remote(X.at[j, :, :, :, :, pl.ds(LANES, LANES)], R.at[j], rp_s, rp_r.at[j],
                      partner)

    def down(i, g):
        j = 5 * g + i
        take(wd_sem.at[j], Wd.at[j])

        for zi in range(4):
            out = jnp.dot(H[zi], Wd[j], preferred_element_type=f32)
            w = wb[zi]
            out = out * jnp.concatenate([w, w, w, w], axis=1)
            X[j, zi] = out.astype(bf16).reshape(4, 4, 16, 512)
        rp_copy(j).start()

    def chip_sum(j):
        rp_copy(j).wait_recv()

        def rows(zi):
            X[j, zi, :, :, :, 0:LANES] += R[j, zi]

        loop(0, 4, rows)

    def plane_of(g, j, at, half=None):
        a = ORDER[g][2]
        rest = [b for b in AX if b != a]
        spec = {b: slice(None) for b in AX}
        spec[a] = at
        if half is not None:
            spec[rest[0]] = pl.ds(2 * half, 2)
        return X.at[j, spec["z"], spec["x"], spec["y"], :, pl.ds(0, LANES)]

    def rs_copy(g, kind, j):
        a = ORDER[g][2]
        p = me[a]
        if kind < 2:
            src, dst = plane_of(g, j, mod4(p + 2), kind), RA1.at[kind, j]
        else:
            src, dst = plane_of(g, j, mod4(p + (1 if kind == 2 else -1))), RA2.at[kind - 2, j]
        return remote(src, dst, rs_s.at[kind // 2], rs_r.at[j, kind // 2],
                      peer(a, 1 if kind % 2 == 0 else -1))

    def line_of(g, stage, j, at):
        if stage == 0:
            rest = [b for b in AX if b != ORDER[g][2]]
            return T.at[j, at] if rest[0] == ORDER[g][1] else T.at[j, :, at]
        return U.at[j, at]

    def rb_copy(g, stage, q, j):
        a = ORDER[g][1 - stage]
        src = line_of(g, stage, j, mod4(me[a] + PEERS[q]))
        return remote(src, (RB, RC)[stage].at[q, j], rb_s.at[stage], rb_r.at[j, stage],
                      peer(a, PEERS[q]))

    def rs_first(g, j):
        for kind in range(2):
            rs_copy(g, kind, j).start()

    def rs_second(g, j):
        p = me[ORDER[g][2]]
        take(rs_r.at[j, 0], RA1.at[:, j])
        for kind in range(2):
            ref = plane_of(g, j, mod4(p + (1 if kind == 0 else -1)), kind)
            ref[...] += RA1[kind, j]
            rs_copy(g, kind + 2, j).start()

    def rs_last(g, j):
        take(rs_r.at[j, 1], RA2.at[:, j])
        total = (plane_of(g, j, me[ORDER[g][2]])[...].astype(f32) + RA2[0, j].astype(f32)
                 + RA2[1, j].astype(f32))
        T[j] = total.astype(bf16)

    def rb_start(g, stage, j):
        for q in range(3):
            rb_copy(g, stage, q, j).start()

    def rb_last(g, stage, j):
        buf = (RB, RC)[stage]
        take(rb_r.at[j, stage], buf.at[:, j])
        total = line_of(g, stage, j, me[ORDER[g][1 - stage]])[...].astype(f32)
        for q in range(3):
            total = total + buf[q, j].astype(f32)
        if stage == 0:
            U[j] = total.astype(bf16)
            return
        first = c == 0
        mine = jnp.where(first, total[0:8], total[8:16])
        FS[j] = jnp.where(first, total[8:16], total[0:8])
        moe_ref[:, pl.ds(pl.multiple_of(c * HALF + j * LANES, LANES), LANES)] = mine.astype(bf16)

    def co_out():
        return pltpu.make_async_copy(co_ref, co_hbm.at[0], io_sem.at[5])

    def hand_over():
        length = jnp.int32(0)
        for q in range(32):
            length = jnp.where(plan_ref[q] == dec, plen_ref[q], length)

        @pl.when(serves)
        def _():
            take(c_sem.at[3], C2.at[pl.ds(0, PIECES - 1)])

        @pl.when(jnp.logical_not(serves))
        def _():
            take(c_sem.at[3], C2.at[pl.ds(0, PIECES)])


        def mask_rows(k):
            pos = y * 256 + lax.broadcasted_iota(jnp.int32, (48, 256), 1)
            kept = co_ref[piece(k), :].astype(f32)
            co_ref[piece(k), :] = jnp.where(pos < length, kept, 0.0).astype(bf16)

        loop(0, PIECES, mask_rows)
        co_out().start()

    def rs_step(i):
        @pl.when(i == 4)
        def _():
            hand_over()

        for g in range(3):
            @pl.when(valid(i, g))
            def _():
                down(i, g)

            ib, gb = (i, g - 1) if g else (i - 1, 2)

            @pl.when(valid(ib, gb))
            def _():
                chip_sum(5 * gb + ib)
                rs_first(gb, 5 * gb + ib)

            @pl.when(valid(ib - 1, gb))
            def _():
                rs_second(gb, 5 * gb + ib - 1)

            @pl.when(valid(ib - 2, gb))
            def _():
                rs_last(gb, 5 * gb + ib - 2)
                rb_start(gb, 0, 5 * gb + ib - 2)

            @pl.when(valid(ib - 3, gb))
            def _():
                rb_last(gb, 0, 5 * gb + ib - 3)
                rb_start(gb, 1, 5 * gb + ib - 3)

            @pl.when(valid(ib - 4, gb))
            def _():
                rb_last(gb, 1, 5 * gb + ib - 4)

    loop(0, 10, rs_step)

    fo = remote(FS, FR, fo_sem.at[0], fo_sem.at[1], partner)
    fo.start()

    @pl.when(serves)
    def _():
        take(c_sem.at[0], C2.at[pl.ds(0, PIECES - 1)])
        take(c_sem.at[2], C2.at[pl.ds(0, 15)])

    @pl.when(jnp.logical_not(serves))
    def _():
        take(c_sem.at[0], C2.at[pl.ds(0, PIECES)])

    take(rp_s, R)
    take(rs_s.at[0], RA1)
    take(rs_s.at[1], RA2)
    take(rb_s.at[0], RB)
    take(rb_s.at[1], RC)
    fo.wait()
    for j in range(NOUT):
        moe_ref[:, pl.ds(pl.multiple_of((1 - c) * HALF + j * LANES, LANES), LANES)] = (
            FR[j].astype(bf16))
    moe_out = pltpu.make_async_copy(moe_ref, moe_hbm, io_sem.at[6])
    moe_out.start()
    co_out().wait()
    moe_out.wait()


def body(
    hidden_states, gate_scores, expert_ids, w_gate, w_up, w_down, prefill_cache, plan, prompt_len
):
    hbm = pl.BlockSpec(memory_space=pl.ANY)
    dma = pltpu.SemaphoreType.DMA
    moe, handed = pl.pallas_call(
        kernel,
        out_shape=(
            jax.ShapeDtypeStruct((8, 7168), bf16),
            jax.ShapeDtypeStruct((1, 576, 256), bf16),
        ),
        in_specs=[hbm] * 9,
        out_specs=(hbm, hbm),
        scratch_shapes=[
            pltpu.VMEM((NCH, 4, 4, 4, 16, 512), bf16),
            pltpu.VMEM((2, 16, NCH * LANES), bf16),
            pltpu.VMEM((16, NCH * LANES), bf16),
            pltpu.VMEM((SLOTS, 512, 1024), bf16),
            pltpu.VMEM((NOUT, 512, 512), bf16),
            pltpu.VMEM((4, 256, 1024), f32),
            pltpu.VMEM((4, 256, 512), bf16),
            pltpu.VMEM((4, 256, 128), f32),
            pltpu.VMEM((NOUT, 4, 4, 4, 16, LANES), bf16),
            pltpu.VMEM((2, NOUT, 2, 4, 16, LANES), bf16),
            pltpu.VMEM((2, NOUT, 4, 4, 16, LANES), bf16),
            pltpu.VMEM((NOUT, 4, 4, 16, LANES), bf16),
            pltpu.VMEM((3, NOUT, 4, 16, LANES), bf16),
            pltpu.VMEM((NOUT, 4, 16, LANES), bf16),
            pltpu.VMEM((3, NOUT, 16, LANES), bf16),
            pltpu.VMEM((NOUT, 8, LANES), f32),
            pltpu.VMEM((NOUT, 8, LANES), f32),
            pltpu.VMEM((32, 48, 256), bf16),
            pltpu.VMEM((16, 48, 256), bf16),
            pltpu.SMEM((16,), jnp.int32),
            pltpu.SMEM((32,), jnp.int32),
            pltpu.SMEM((32,), jnp.int32),
            pltpu.VMEM((8, 8), f32),
            pltpu.VMEM((8, 8), jnp.int32),
            pltpu.VMEM((8, 7168), bf16),
            pltpu.VMEM((8, 7168), bf16),
            pltpu.VMEM((576, 256), bf16),
            dma((7,)),
            dma((2,)),
            dma((2,)), dma((2, 2)),
            dma, dma((NCH, 2)),
            dma, dma((NOUT,)),
            dma((SLOTS,)), dma((NOUT,)),
            dma, dma((NOUT,)),
            dma((2,)), dma((NOUT, 2)),
            dma((2,)), dma((NOUT, 2)),
            dma((2,)),
            dma((5,)),
            dma((2,)),
        ],
        compiler_params=pltpu.CompilerParams(
            collective_id=0, has_side_effects=True, vmem_limit_bytes=60 * 1024 * 1024),
        cost_estimate=pl.CostEstimate(
            flops=22_500_000_000, bytes_accessed=23_000_000, transcendentals=524288),
    )(plan, prompt_len, gate_scores, expert_ids, hidden_states,
      jnp.swapaxes(prefill_cache, 1, 2), w_gate, w_up, w_down)

    def hand_on(moe_in, handed_in, moe_out, handed_out):
        moe_out[...] = moe_in[...]
        handed_out[...] = handed_in[...]

    vm = pl.BlockSpec(memory_space=pltpu.VMEM)
    moe, handed = pl.pallas_call(
        hand_on,
        out_shape=(
            jax.ShapeDtypeStruct((8, 7168), bf16),
            jax.ShapeDtypeStruct((1, 576, 256), bf16),
        ),
        in_specs=[vm, vm],
        out_specs=(vm, vm),
        cost_estimate=pl.CostEstimate(flops=0, bytes_accessed=820_000, transcendentals=0),
    )(moe, handed)
    return moe, jnp.swapaxes(handed, 1, 2)


def solution(mesh):
    in_specs = (
        P(("dec", "seq"), None),
        P(("dec", "seq"), None),
        P(("dec", "seq"), None),
        P("dec", None, "seq"),
        P("dec", None, "seq"),
        P("dec", "seq", None),
        P("dec", "seq", None),
        P(),
        P(),
    )
    out_specs = (P(("dec", "seq"), None), P("dec", "seq", None))
    return jax.shard_map(body, mesh=mesh, in_specs=in_specs, out_specs=out_specs, check_vma=False)
```

time: 311 us -> 109 us (0.35)
  waiting for transfers between devices: 176 us -> 0 us
  Pallas kernels: 0 us -> 108 us
  local copies, waits for them, and re-layouts: 40.9 us -> 0 us
  other arithmetic: 29.9 us -> 0 us
  matrix products: 27.1 us -> 0 us
  starting transfers between devices: 20.5 us -> 0 us
  between operations: 14.2 us -> 0.64 us
    all_to_all x2 -> x0, waiting for transfers between devices: 175 us -> none  [the longest x1 92.3 us: body(): lax.all_to_all(copies, ('dec', 'seq'), split_axis=0, concat_axis=0, tiled...]
    pallas_call x0 -> x2, Pallas kernels: none -> 108 us  [the longest x1 107 us: body(): pl.pallas_call(kernel, out_shape=(jax.ShapeDtypeStruct((8, 7168), bf16),...]
    reshape x4 -> x0, local copies, waits for them, and re-layouts: 28.7 us -> none  [the longest x1 12.7 us: body(): partial_value = partial_value.reshape(n_dec * n_seq, capacity, features)]
    reduce_sum x8 -> x0, other arithmetic: 27.4 us -> none  [the longest x1 14.8 us: body(): received = jnp.sum(kept, axis=0, keepdims=True)]
    dot_general x4 -> x0, matrix products: 27.1 us -> none  [the longest x1 9.59 us: body(): jnp.dot(hidden, down_local, preferred_element_type=jnp.float32)]
    all_to_all x2 -> x0, starting transfers between devices: 20.5 us -> none  [the longest x1 11.9 us: body(): lax.all_to_all(copies, ('dec', 'seq'), split_axis=0, concat_axis=0, tiled...]
    broadcast_in_dim x2 -> x0, local copies, waits for them, and re-layouts: 8.3 us -> none  [body(): jnp.broadcast_to(buffer[:, None], (n_dec, n_seq, capacity, features))]
  transfers between devices with their start and end apart: 3 -> 0, of which waited for: 2 -> 0; matrix products, arithmetic and copies ran while one was open for 23% -> 0% of each run, Pallas kernels for 0% -> 0%
where the time goes in v2:
time: 109 us
  Pallas kernels  108 us (99%)
    pallas_call x1, Pallas kernels, body(): pl.pallas_call(kernel, out_shape=(jax.ShapeDtypeStruct((8, 7168), bf16),...  107 us

profile of v2, /device:TPU:1, one launch (start us, length us, event | category | flops | bytes accessed | tf_op | source)
XLA Modules:
  0.0 109.1 jit_solution(566897216562749903)
XLA Ops:
  0.6 106.7 %shard_map.104 = (bf16[8,7168]{1,0:T(8,128)(2,1)}, bf16[1,576,256]{2,1,0:T(8,128)(2,1)}) custom-call(s32[32]{0:T(128)} %plan_hbm.1, s32[32]{0:T(128)} %plen_hbm.1, f32[8,8]{1,0:T(8,128)} %scores_hbm.1, s32[8,8]{1,0:T(8,128)} %ids_hbm.1, bf16[8,7168]{1,0:T(8,128)(2,1)} %hid_hbm.1, bf16[1,576,256]{2,1,0:T(8,128)(2,1)} %bitcast.2, ...), custom_call_target="tpu_custom_call" | custom-call | flops 22499999744 | bytes 23000000 | tf_op jit(solution)/shard_map/pallas_call | solution.py:526
  107.4 1.8 %shard_map.105 = (bf16[8,7168]{1,0:T(8,128)(2,1)}, bf16[1,576,256]{2,1,0:T(8,128)(2,1)}) custom-call(bf16[8,7168]{1,0:T(8,128)(2,1)} %get-tuple-element.6.moe_in, bf16[1,576,256]{2,1,0:T(8,128)(2,1)} %get-tuple-element.7.handed_in), custom_call_target="tpu_custom_call" | custom-call | bytes 820000 | tf_op jit(solution)/shard_map/pallas_call | solution.py:587

commit v3 on v2

--- a/solution.py
+++ b/solution.py
@@ -33,10 +33,10 @@
 def kernel(
     plan_hbm, plen_hbm, scores_hbm, ids_hbm, hid_hbm, cache_ref, wg_ref, wu_ref, wd_ref,
     moe_hbm, co_hbm,
-    X, xin, xr, Wgu, Wd, acc, H, wb, R, RA1, RA2, T, RB, U, RC, FS, FR, C1, C2, order_ref,
+    X, xin, xr, ext, extr, Wgu, Wd, acc, H, wb, R, RA1, RA2, T, RB, U, RC, RT, FS, FR, C1, C2, order_ref,
     plan_ref, plen_ref, scores_ref, ids_ref, hid_ref, moe_ref, co_ref, io_sem,
     x_sem, ag_s, ag_r, ag3_s, ag3_r, agp_s, agp_r, w_sem, wd_sem,
-    rp_s, rp_r, rs_s, rs_r, rb_s, rb_r, fo_sem, c_sem, cp_sem,
+    rp_s, rp_r, rs_s, rs_r, rb_s, rb_r, rt_s, rt_r, fo_sem, c_sem, cp_sem,
 ):
     dec = lax.axis_index("dec")
     y = lax.axis_index("seq")
@@ -52,6 +52,12 @@
         pos[a] = mod4(me[a] + d)
         return dev(pos, c)
 
+    def mate(a, b, o):
+        pos = dict(me)
+        pos[a] = mod4(me[a] + o // 4)
+        pos[b] = mod4(me[b] + o % 4)
+        return dev(pos, c)
+
     partner = dev(me, 1 - c)
 
     def plane_id(o):
@@ -72,9 +78,46 @@
     barrier = pltpu.get_barrier_semaphore()
     for o in range(1, 16):
         pl.semaphore_signal(barrier, inc=1, device_id=plane_id(o), device_id_type=MESH)
-    for d in (1, -1, 2):
-        pl.semaphore_signal(barrier, inc=1, device_id=peer("y", d), device_id_type=MESH)
+    for o in range(4, 16):
+        pl.semaphore_signal(barrier, inc=1, device_id=mate("y", "x", o), device_id_type=MESH)
+    for o in range(5, 16):
+        if o % 4:
+            pl.semaphore_signal(barrier, inc=1, device_id=mate("z", "y", o), device_id_type=MESH)
     pl.semaphore_signal(barrier, inc=1, device_id=partner, device_id_type=MESH)
+
+    def piece(k):
+        return pl.ds(pl.multiple_of(k * 48, 16), 48)
+
+    serves = chip < PIECES
+
+    def c1_copy(o):
+        to = lax.rem(chip + o, 16)
+        return remote(cache_ref.at[0, piece(to), :], C1.at[chip], c_sem.at[0], c_sem.at[1],
+                      plane_id(o))
+
+    def c2_copy(o):
+        to = lax.rem(chip + o, 16)
+        return remote(C2.at[to], co_ref.at[piece(chip), :], c_sem.at[2], c_sem.at[3],
+                      plane_id(o))
+
+    def cp_copy():
+        return remote(C1.at[pl.ds(0, 16)], C1.at[pl.ds(16, 16)], cp_sem.at[0], cp_sem.at[1],
+                      partner)
+
+    def c1_own():
+        return pltpu.make_async_copy(cache_ref.at[0, piece(chip), :], C1.at[chip], c_sem.at[4])
+
+    def cache_start():
+        def c1_start(o):
+            @pl.when(lax.rem(chip + o, 16) < PIECES)
+            def _():
+                c1_copy(o).start()
+
+        loop(1, 16, c1_start)
+
+        @pl.when(serves)
+        def _():
+            c1_own().start()
 
     def w_copies(i, g):
         slot = lax.rem(3 * i + g, SLOTS)
@@ -106,7 +149,22 @@
             for cp in w_copies(i, g):
                 cp.start()
 
-    for cp in loads:
+    def two(v):
+        mine = lax.broadcasted_iota(jnp.int32, (16, v.shape[1]), 0) // 8 == c
+        return jnp.where(mine, jnp.concatenate([v, v], axis=0), 0.0).astype(bf16)
+
+    loads[0].wait()
+    for h in range(2):
+        for t in range(NOUT):
+            lane = slice(h * HALF + t * LANES, h * HALF + (t + 1) * LANES)
+            xin[h, :, t * LANES:(t + 1) * LANES] = two(hid_ref[:, lane].astype(f32))
+
+    pl.semaphore_wait(barrier, 37)
+
+    swap = remote(xin.at[1 - c], xr, x_sem.at[0], x_sem.at[1], partner)
+    swap.start()
+    cache_start()
+    for cp in loads[1:]:
         cp.wait()
     score = 1.0 / (1.0 + jnp.exp(-scores_ref[...]))
     weight = 2.5 * score / jnp.sum(score, axis=1, keepdims=True)
@@ -121,23 +179,12 @@
     part = lane8 // 32
     extra = jnp.where(part == 0, hi, jnp.where(part == 1, mid, jnp.where(part == 2, low, 0.0)))
 
-    def two(v):
-        mine = lax.broadcasted_iota(jnp.int32, (16, v.shape[1]), 0) // 8 == c
-        return jnp.where(mine, jnp.concatenate([v, v], axis=0), 0.0).astype(bf16)
-
-    for h in range(2):
-        for t in range(NOUT):
-            lane = slice(h * HALF + t * LANES, h * HALF + (t + 1) * LANES)
-            xin[h, :, t * LANES:(t + 1) * LANES] = two(hid_ref[:, lane].astype(f32))
-        xin[h, :, HALF:HALF + 128] = two(extra)
-        xin[h, :, HALF + 128:HALF + 256] = jnp.zeros((16, 128), bf16)
-
-    pl.semaphore_wait(barrier, 19)
-
-    swap = remote(xin.at[1 - c], xr, x_sem.at[0], x_sem.at[1], partner)
-    swap.start()
+    ext[...] = two(extra)
+    swap2 = remote(ext, extr, x_sem.at[2], x_sem.at[3], partner)
+    swap2.start()
+
     swap.wait()
-    for j in range(NCH):
+    for j in range(NOUT):
         lane = slice(j * LANES, (j + 1) * LANES)
         X[j, me["z"], me["x"], me["y"], :, 0:LANES] = xin[c, :, lane] + xr[:, lane]
 
@@ -169,25 +216,6 @@
             X.at[j, :, :, :, :, pl.ds(0, LANES)], X.at[j, :, :, :, :, pl.ds(LANES, LANES)],
             agp_s, agp_r.at[j], partner)
 
-    def piece(k):
-        return pl.ds(pl.multiple_of(k * 48, 16), 48)
-
-    serves = chip < PIECES
-
-    def c1_copy(o):
-        to = lax.rem(chip + o, 16)
-        return remote(cache_ref.at[0, piece(to), :], C1.at[chip], c_sem.at[0], c_sem.at[1],
-                      plane_id(o))
-
-    def c2_copy(o):
-        to = lax.rem(chip + o, 16)
-        return remote(C2.at[to], co_ref.at[piece(chip), :], c_sem.at[2], c_sem.at[3],
-                      plane_id(o))
-
-    def cp_copy():
-        return remote(C1.at[pl.ds(0, 16)], C1.at[pl.ds(16, 16)], cp_sem.at[0], cp_sem.at[1],
-                      partner)
-
     def ag_all(stage, part, act):
         for g in range(3):
             for q in range(3):
@@ -208,13 +236,15 @@
              X.at[5 * g + i, spec["z"], spec["x"], spec["y"], :, pl.ds(0, LANES)])
 
     ag_all(0, 0, start)
+    swap2.wait()
+    X[14, me["z"], me["x"], me["y"], :, 0:128] = ext[...] + extr[...]
+    X[14, me["z"], me["x"], me["y"], :, 128:256] = jnp.zeros((16, 128), bf16)
     ag_all(0, 1, start)
 
     def wd_start(j):
         for cp in wd_copies(j):
             cp.start()
 
-    loop(0, NOUT, wd_start)
     acc[...] = jnp.zeros_like(acc)
 
     def find(k):
@@ -229,20 +259,6 @@
     ag_take(0, 1)
     ag_all(1, 1, start)
 
-    def c1_own():
-        return pltpu.make_async_copy(cache_ref.at[0, piece(chip), :], C1.at[chip], c_sem.at[4])
-
-    def c1_start(o):
-        @pl.when(lax.rem(chip + o, 16) < PIECES)
-        def _():
-            c1_copy(o).start()
-
-    loop(1, 16, c1_start)
-
-    @pl.when(serves)
-    def _():
-        c1_own().start()
-
     loop(0, 16, find)
 
     def ag3_start(i):
@@ -297,6 +313,10 @@
             @pl.when(valid(i - 1, g))
             def _():
                 ag_partner(5 * g + i - 1).start()
+
+        @pl.when(i == 1)
+        def _():
+            loop(0, NOUT, wd_start)
 
         @pl.when(i == 2)
         def _():
@@ -347,12 +367,14 @@
         j = 5 * g + i
         take(wd_sem.at[j], Wd.at[j])
 
-        for zi in range(4):
-            out = jnp.dot(H[zi], Wd[j], preferred_element_type=f32)
-            w = wb[zi]
-            out = out * jnp.concatenate([w, w, w, w], axis=1)
-            X[j, zi] = out.astype(bf16).reshape(4, 4, 16, 512)
-        rp_copy(j).start()
+        w = wb[...].reshape(1024, 128)
+        w = jnp.concatenate([w, w], axis=1)
+        for h in (1, 0):
+            lane = slice(h * LANES, (h + 1) * LANES)
+            out = jnp.dot(H[...].reshape(1024, 512), Wd[j, :, lane], preferred_element_type=f32)
+            X[j, :, :, :, :, lane] = (out * w).astype(bf16).reshape(4, 4, 4, 16, LANES)
+            if h:
+                rp_copy(j).start()
 
     def chip_sum(j):
         rp_copy(j).wait_recv()
@@ -393,6 +415,33 @@
         return remote(src, (RB, RC)[stage].at[q, j], rb_s.at[stage], rb_r.at[j, stage],
                       peer(a, PEERS[q]))
 
+    def tail_piece(g, j, o):
+        a1, a2, a3 = ORDER[g]
+        at = {a1: mod4(me[a1] + o // 4), a2: mod4(me[a2] + o % 4)}
+        rest = [b for b in AX if b != a3]
+        return T.at[j, at[rest[0]], at[rest[1]]]
+
+    def tail_start(g, j):
+        def one(q):
+            o = 16 - q
+            remote(tail_piece(g, j, o), RT.at[g, o - 1], rt_s, rt_r.at[g],
+                   mate(ORDER[g][0], ORDER[g][1], o)).start()
+
+        loop(1, 16, one)
+
+    def tail_last(g, j):
+        take(rt_r.at[g], RT.at[g])
+        total = tail_piece(g, j, 0)[...].astype(f32)
+        for o in range(15):
+            total = total + RT[g, o].astype(f32)
+        finish(j, total)
+
+    def tail(i, g):
+        return i == (3 if g == 2 else 4)
+
+    def early(i, g):
+        return (i >= 0) & (i < (3 if g == 2 else 4))
+
     def rs_first(g, j):
         for kind in range(2):
             rs_copy(g, kind, j).start()
@@ -423,7 +472,10 @@
             total = total + buf[q, j].astype(f32)
         if stage == 0:
             U[j] = total.astype(bf16)
-            return
+        else:
+            finish(j, total)
+
+    def finish(j, total):
         first = c == 0
         mine = jnp.where(first, total[0:8], total[8:16])
         FS[j] = jnp.where(first, total[8:16], total[0:8])
@@ -466,30 +518,41 @@
 
             ib, gb = (i, g - 1) if g else (i - 1, 2)
 
+            @pl.when(early(ib - 4, gb))
+            def _():
+                rb_last(gb, 1, 5 * gb + ib - 4)
+
+            @pl.when(tail(ib - 3, gb))
+            def _():
+                tail_last(gb, 5 * gb + ib - 3)
+
+            @pl.when(early(ib - 3, gb))
+            def _():
+                rb_last(gb, 0, 5 * gb + ib - 3)
+                rb_start(gb, 1, 5 * gb + ib - 3)
+
+            @pl.when(valid(ib - 2, gb))
+            def _():
+                rs_last(gb, 5 * gb + ib - 2)
+
+            @pl.when(early(ib - 2, gb))
+            def _():
+                rb_start(gb, 0, 5 * gb + ib - 2)
+
+            @pl.when(tail(ib - 2, gb))
+            def _():
+                tail_start(gb, 5 * gb + ib - 2)
+
+            @pl.when(valid(ib - 1, gb))
+            def _():
+                rs_second(gb, 5 * gb + ib - 1)
+
             @pl.when(valid(ib, gb))
             def _():
                 chip_sum(5 * gb + ib)
                 rs_first(gb, 5 * gb + ib)
 
-            @pl.when(valid(ib - 1, gb))
-            def _():
-                rs_second(gb, 5 * gb + ib - 1)
-
-            @pl.when(valid(ib - 2, gb))
-            def _():
-                rs_last(gb, 5 * gb + ib - 2)
-                rb_start(gb, 0, 5 * gb + ib - 2)
-
-            @pl.when(valid(ib - 3, gb))
-            def _():
-                rb_last(gb, 0, 5 * gb + ib - 3)
-                rb_start(gb, 1, 5 * gb + ib - 3)
-
-            @pl.when(valid(ib - 4, gb))
-            def _():
-                rb_last(gb, 1, 5 * gb + ib - 4)
-
-    loop(0, 10, rs_step)
+    loop(0, 8, rs_step)
 
     fo = remote(FS, FR, fo_sem.at[0], fo_sem.at[1], partner)
     fo.start()
@@ -506,8 +569,9 @@
     take(rp_s, R)
     take(rs_s.at[0], RA1)
     take(rs_s.at[1], RA2)
-    take(rb_s.at[0], RB)
-    take(rb_s.at[1], RC)
+    take(rb_s.at[0], RB.at[:, pl.ds(0, NOUT - 3)])
+    take(rb_s.at[1], RC.at[:, pl.ds(0, NOUT - 3)])
+    take(rt_s, RT)
     fo.wait()
     for j in range(NOUT):
         moe_ref[:, pl.ds(pl.multiple_of((1 - c) * HALF + j * LANES, LANES), LANES)] = (
@@ -533,8 +597,10 @@
         out_specs=(hbm, hbm),
         scratch_shapes=[
             pltpu.VMEM((NCH, 4, 4, 4, 16, 512), bf16),
-            pltpu.VMEM((2, 16, NCH * LANES), bf16),
-            pltpu.VMEM((16, NCH * LANES), bf16),
+            pltpu.VMEM((2, 16, HALF), bf16),
+            pltpu.VMEM((16, HALF), bf16),
+            pltpu.VMEM((16, 128), bf16),
+            pltpu.VMEM((16, 128), bf16),
             pltpu.VMEM((SLOTS, 512, 1024), bf16),
             pltpu.VMEM((NOUT, 512, 512), bf16),
             pltpu.VMEM((4, 256, 1024), f32),
@@ -547,6 +613,7 @@
             pltpu.VMEM((3, NOUT, 4, 16, LANES), bf16),
             pltpu.VMEM((NOUT, 4, 16, LANES), bf16),
             pltpu.VMEM((3, NOUT, 16, LANES), bf16),
+            pltpu.VMEM((3, 15, 16, LANES), bf16),
             pltpu.VMEM((NOUT, 8, LANES), f32),
             pltpu.VMEM((NOUT, 8, LANES), f32),
             pltpu.VMEM((32, 48, 256), bf16),
@@ -560,7 +627,7 @@
             pltpu.VMEM((8, 7168), bf16),
             pltpu.VMEM((576, 256), bf16),
             dma((7,)),
-            dma((2,)),
+            dma((4,)),
             dma((2,)), dma((2, 2)),
             dma, dma((NCH, 2)),
             dma, dma((NOUT,)),
@@ -568,6 +635,7 @@
             dma, dma((NOUT,)),
             dma((2,)), dma((NOUT, 2)),
             dma((2,)), dma((NOUT, 2)),
+            dma, dma((3,)),
             dma((2,)),
             dma((5,)),
             dma((2,)),

time: 109 us -> 109 us (level)
  no operation moved by 1% of the time
where the time goes in v3:
time: 109 us
  Pallas kernels  108 us (99%)
    pallas_call x1, Pallas kernels, body(): pl.pallas_call(kernel, out_shape=(jax.ShapeDtypeStruct((8, 7168), bf16),...  106 us

profile of v3, /device:TPU:1, one launch (start us, length us, event | category | flops | bytes accessed | tf_op | source)
XLA Modules:
  0.0 108.6 jit_solution(10058704983193301453)
XLA Ops:
  0.6 106.2 %shard_map.104 = (bf16[8,7168]{1,0:T(8,128)(2,1)}, bf16[1,576,256]{2,1,0:T(8,128)(2,1)}) custom-call(s32[32]{0:T(128)} %plan_hbm.1, s32[32]{0:T(128)} %plen_hbm.1, f32[8,8]{1,0:T(8,128)} %scores_hbm.1, s32[8,8]{1,0:T(8,128)} %ids_hbm.1, bf16[8,7168]{1,0:T(8,128)(2,1)} %hid_hbm.1, bf16[1,576,256]{2,1,0:T(8,128)(2,1)} %bitcast.2, ...), custom_call_target="tpu_custom_call" | custom-call | flops 22499999744 | bytes 23000000 | tf_op jit(solution)/shard_map/pallas_call | solution.py:590
  106.8 1.8 %shard_map.105 = (bf16[8,7168]{1,0:T(8,128)(2,1)}, bf16[1,576,256]{2,1,0:T(8,128)(2,1)}) custom-call(bf16[8,7168]{1,0:T(8,128)(2,1)} %get-tuple-element.6.moe_in, bf16[1,576,256]{2,1,0:T(8,128)(2,1)} %get-tuple-element.7.handed_in), custom_call_target="tpu_custom_call" | custom-call | bytes 820000 | tf_op jit(solution)/shard_map/pallas_call | solution.py:655

commit v4 on v3

--- a/solution.py
+++ b/solution.py
@@ -211,10 +211,13 @@
         return remote(ref, ref, ag3_s, ag3_r.at[j, kind // 2],
                       peer(a, 1 if kind % 2 == 0 else -1))
 
-    def ag_partner(j):
-        return remote(
-            X.at[j, :, :, :, :, pl.ds(0, LANES)], X.at[j, :, :, :, :, pl.ds(LANES, LANES)],
-            agp_s, agp_r.at[j], partner)
+    def ag_partner(g, i, d):
+        j = 5 * g + i
+        spec = {b: slice(None) for b in AX}
+        spec[ORDER[g][2]] = mod4(me[ORDER[g][2]] + d)
+        at = (j, spec["z"], spec["x"], spec["y"], slice(None))
+        return remote(X.at[(*at, pl.ds(0, LANES))], X.at[(*at, pl.ds(LANES, LANES))],
+                      agp_s, agp_r.at[j], partner)
 
     def ag_all(stage, part, act):
         for g in range(3):
@@ -296,6 +299,11 @@
                 for kind in range(2):
                     ag3_copy(g, kind + 2, i).start()
 
+            @pl.when(valid(i, g))
+            def _():
+                for d in (0, -1, 1):
+                    ag_partner(g, i, d).start()
+
             @pl.when(i + 2 < 5)
             def _():
                 for kind in range(2):
@@ -303,7 +311,8 @@
 
             @pl.when(valid(i - 2, g))
             def _():
-                ag_partner(5 * g + i - 2).wait_recv()
+                j = 5 * g + i - 2
+                take(agp_r.at[j], X.at[j, :, :, :, :, pl.ds(LANES, LANES)])
                 gate_up(i - 2, g)
 
             @pl.when((i >= 1) & (i < 6))
@@ -312,7 +321,7 @@
 
             @pl.when(valid(i - 1, g))
             def _():
-                ag_partner(5 * g + i - 1).start()
+                ag_partner(g, i - 1, 2).start()
 
         @pl.when(i == 1)
         def _():

time: 109 us -> 109 us (level)
  no operation moved by 1% of the time
where the time goes in v4:
time: 109 us
  Pallas kernels  108 us (99%)
    pallas_call x1, Pallas kernels, body(): pl.pallas_call(kernel, out_shape=(jax.ShapeDtypeStruct((8, 7168), bf16),...  107 us

profile of v4, /device:TPU:1, one launch (start us, length us, event | category | flops | bytes accessed | tf_op | source)
XLA Modules:
  0.0 109.1 jit_solution(12145196215862352604)
XLA Ops:
  0.6 106.7 %shard_map.104 = (bf16[8,7168]{1,0:T(8,128)(2,1)}, bf16[1,576,256]{2,1,0:T(8,128)(2,1)}) custom-call(s32[32]{0:T(128)} %plan_hbm.1, s32[32]{0:T(128)} %plen_hbm.1, f32[8,8]{1,0:T(8,128)} %scores_hbm.1, s32[8,8]{1,0:T(8,128)} %ids_hbm.1, bf16[8,7168]{1,0:T(8,128)(2,1)} %hid_hbm.1, bf16[1,576,256]{2,1,0:T(8,128)(2,1)} %bitcast.2, ...), custom_call_target="tpu_custom_call" | custom-call | flops 22499999744 | bytes 23000000 | tf_op jit(solution)/shard_map/pallas_call | solution.py:599
  107.3 1.8 %shard_map.105 = (bf16[8,7168]{1,0:T(8,128)(2,1)}, bf16[1,576,256]{2,1,0:T(8,128)(2,1)}) custom-call(bf16[8,7168]{1,0:T(8,128)(2,1)} %get-tuple-element.6.moe_in, bf16[1,576,256]{2,1,0:T(8,128)(2,1)} %get-tuple-element.7.handed_in), custom_call_target="tpu_custom_call" | custom-call | bytes 820000 | tf_op jit(solution)/shard_map/pallas_call | solution.py:664
